TPU v7x, 512 devices: a whole 4x4x16 slice. The times are simulated.
512 devices in a mesh: dp: 16 (over y, z_lo), factor: 32 (over z_hi, x, core).
Axes of the slice: x: 4, y: 4, z: 16 (z_hi: 4, z_lo: 4; z = z_hi * 4 + z_lo), core: 2. Of those that a mesh axis runs over, the one named last changes fastest.
Arguments:
- acts: bfloat16 [2048, 6144], P('dp', 'factor'), may hold values from -6 to 6
- grads_out: bfloat16 [2048, 12288], P('dp', 'factor'), may hold values from -6 to 6
- owners: int32 [136], replicated, may hold values from 0 to 31, as said below
Outputs:
- panel_rows: float32 [32, 6, 128, 512], P('factor', None, 'dp')
- precond_block: float32 [512, 512], P('factor')
Inputs may be any that keep to these rules, and one draw needn't show every extreme that they name: `owners`: each owner holds at most 6 tiles, and one owner holds exactly 6 in every draw.
All inputs are finite; a program needn't handle non-finite values.
Results may differ from a plain program's by a relative error of at most 0.0003.
Values may be sent and summed in bfloat16 or wider, within the bound.
A program may use at most 64 MiB of HBM per device.

v0:
```python
import jax
import jax.numpy as jnp
from jax import lax
from jax.experimental import pallas as pl
from jax.experimental.pallas import tpu as pltpu
from jax.sharding import PartitionSpec as P

D = 6144
PANEL = 512
TILE = 128
NT = 136
TILES_A = (D - PANEL) // TILE
CAP = 6
BLK = 128
GROUPS = 5
FROWS = 48

damping = 0.1
MESH = pl.DeviceIdType.MESH
HIGH = lax.Precision.HIGHEST


def lanes(x, c):
    return jnp.broadcast_to(x[:, :, c:c + 1], x.shape)


def rows8(x, j):
    return jnp.broadcast_to(x[:, j:j + 1, :], x.shape)


def recip(x):
    r = pl.reciprocal(x, approx=True)
    r = r * (2.0 - x * r)
    return r * (2.0 - x * r)


def pair(ba, bb, j):
    p00, p01, p11 = rows8(ba, j), rows8(bb, j), rows8(bb, j + 1)
    det = p00 * p11 - p01 * p01
    r0, rd = recip(p00), recip(det)
    return p00, p01, det, r0, rd


def strip16(x0, x1, w0, w1, c0, sub):
    b0 = [lanes(x0, c0 + j) for j in range(16)]
    b1 = [lanes(x1, c0 + j) for j in range(16)]
    d0 = jnp.ones(x0.shape, jnp.float32)
    d1 = d0
    for j in range(0, 8, 2):
        ba, bb = b0[j], b0[j + 1]
        p00, p01, det, r0, rd = pair(ba, bb, j)
        d0 = jnp.where(sub == j, p00, jnp.where(sub == j + 1, det * r0, d0))
        q = p01 * r0
        m0a = jnp.where(sub > j, ba, 0.0) * r0
        m0b = jnp.where(sub > j + 1, bb * p00 - ba * p01, 0.0) * rd
        m1a = b1[j] * r0
        m1b = (b1[j + 1] * p00 - b1[j] * p01) * rd
        for k in range(j + 2, 16):
            ra = rows8(b0[k], j)
            rb = rows8(b0[k], j + 1) - q * ra
            b0[k] = b0[k] - m0a * ra - m0b * rb
            b1[k] = b1[k] - m1a * ra - m1b * rb
        ra = rows8(x0, j)
        rb = rows8(x0, j + 1) - q * ra
        x0 = x0 - m0a * ra - m0b * rb
        x1 = x1 - m1a * ra - m1b * rb
        ra = rows8(w0, j)
        rb = rows8(w0, j + 1) - q * ra
        w0 = w0 - m0a * ra - m0b * rb
        w1 = w1 - m1a * ra - m1b * rb
    for j in range(0, 8, 2):
        ba, bb = b1[8 + j], b1[9 + j]
        p00, p01, det, r0, rd = pair(ba, bb, j)
        d1 = jnp.where(sub == j, p00, jnp.where(sub == j + 1, det * r0, d1))
        q = p01 * r0
        ma = jnp.where(sub > j, ba, 0.0) * r0
        mb = jnp.where(sub > j + 1, bb * p00 - ba * p01, 0.0) * rd
        for k in range(j + 2, 8):
            ra = rows8(b1[8 + k], j)
            rb = rows8(b1[8 + k], j + 1) - q * ra
            b1[8 + k] = b1[8 + k] - ma * ra - mb * rb
        ra = rows8(x1, j)
        rb = rows8(x1, j + 1) - q * ra
        x1 = x1 - ma * ra - mb * rb
        ra = rows8(w1, j)
        rb = rows8(w1, j + 1) - q * ra
        w1 = w1 - ma * ra - mb * rb
    s0, s1 = lax.rsqrt(d0), lax.rsqrt(d1)
    s0 = s0 * (1.5 - 0.5 * d0 * s0 * s0)
    s1 = s1 * (1.5 - 0.5 * d1 * s1 * s1)
    return x0 * s0, x1 * s1, w0 * s0, w1 * s1


def factor_blocks(x, out):
    sub = lax.broadcasted_iota(jnp.int32, (2, 8, BLK), 1)
    w = jnp.where(lax.broadcasted_iota(jnp.int32, (2, BLK, BLK), 1)
                  == lax.broadcasted_iota(jnp.int32, (2, BLK, BLK), 2), 1.0, 0.0).astype(jnp.float32)
    for i in range(8):
        v0, v1, u0, u1 = strip16(x[:, 0:8], x[:, 8:16], w[:, 0:8], w[:, 8:16], 16 * i, sub)
        out[:, 16 * i:16 * i + 8, :] = u0
        out[:, 16 * i + 8:16 * i + 16, :] = u1
        if i == 7:
            break
        lo = 16 * (i + 1)
        v = jnp.concatenate([v0, v1], 1)
        u = jnp.concatenate([u0, u1], 1)
        vt = jnp.stack([v[0].T, v[1].T])
        nx, nw = x[:, 16:32], w[:, 16:32]
        for j in range(16):
            m = jnp.broadcast_to(vt[:, lo:lo + 16, j:j + 1], nx.shape)
            nx = nx - m * v[:, j:j + 1, :]
            nw = nw - m * u[:, j:j + 1, :]
        if i == 6:
            x, w = nx, nw
            continue
        vu = jnp.concatenate([v, u], 2)
        less = jnp.stack([dot32(vt[n, lo + 16:, :], vu[n], ((1,), (0,))) for n in range(2)])
        x = jnp.concatenate([nx, x[:, 32:] - less[:, :, 0:BLK]], 1)
        w = jnp.concatenate([nw, w[:, 32:] - less[:, :, BLK:]], 1)


def dot32(a, b, dims):
    return lax.dot_general(a, b, (dims, ((), ())), precision=HIGH, preferred_element_type=jnp.float32)


def dot16(a, b, dims):
    return lax.dot_general(a, b, (dims, ((), ())), preferred_element_type=jnp.float32)


def owned_tables(own_ref, d, ids):
    zero = jnp.int32(0)

    def look(t, carry):
        owner = own_ref[t]
        out = []
        for n, *slots in carry:
            hit = owner == ids[len(out)]
            slots = [jnp.where(jnp.logical_and(hit, n == s), t, slots[s]) for s in range(CAP)]
            out.append((n + hit.astype(jnp.int32),) + tuple(slots))
        return tuple(out)

    found = lax.fori_loop(0, NT, look, tuple((zero,) * (CAP + 1) for _ in ids))
    p = lax.div(d, 8)
    tables = []
    for n, *slots in found:
        table = []
        for s in range(CAP):
            t = slots[s]
            half = 2 * (t + 4) + p
            fa = lax.div(half, 3)
            slot_a = lax.div(half - 3 * fa - lax.rem(3 * fa + p, 2), 2)
            tg = jnp.maximum(t - TILES_A, 0) + 4
            fg = lax.div(tg, 3)
            slot_g = 2 + tg - 3 * fg
            act = t < TILES_A
            table.append((
                jnp.where(act, fa, fg), jnp.where(act, slot_a, slot_g),
                act.astype(jnp.int32), (s < n).astype(jnp.int32)))
        tables.append(table)
    return tables


def kernel(own_in, at_in, gr_in, rows_out, pre_out,
           own_ref, act_t, gr, fs, za, pan, feat, z1, mat, inv0, invt, wmat, raw, loc, pack, got, picked,
           s_in, s_p, r_p, s_b, s_c, r_own, s_z, r_blk, s_y, s_far, r_far, s_x, r_x, s_sib, r_sib, s_f, r_f,
           s_lx, s_ls, r_l, s_g, r_g):
    d = lax.axis_index("dp")
    f = lax.axis_index("factor")
    y, zl = lax.div(d, 4), lax.rem(d, 4)
    role, zh, core = lax.rem(f, 8), lax.div(f, 8), lax.rem(f, 2)
    xx = lax.div(role, 2)
    base = f - role
    sib = f + 1 - 2 * core
    scale = 1.0 / 2048.0

    def z_peer(k):
        return lax.rem(f + 8 * k, 32)

    def x_peer(k):
        return base + 2 * lax.rem(xx + k, 4) + core

    def copy(src, dst, send, recv, to):
        return pltpu.make_async_remote_copy(
            src_ref=src, dst_ref=dst, send_sem=send, recv_sem=recv,
            device_id=to, device_id_type=MESH)

    fetch = (
        pltpu.make_async_copy(at_in, act_t, s_in.at[0]),
        pltpu.make_async_copy(gr_in, gr, s_in.at[1]),
        pltpu.make_async_copy(own_in, own_ref, s_in.at[2]),
    )
    for c in fetch:
        c.start()

    barrier = pltpu.get_barrier_semaphore()
    for k in range(1, 16):
        pl.semaphore_signal(barrier, inc=1, device_id=(lax.rem(d + k, 16), f), device_id_type=MESH)
    for k in range(1, 4):
        pl.semaphore_signal(barrier, inc=1, device_id=(d, z_peer(k)), device_id_type=MESH)
        pl.semaphore_signal(barrier, inc=1, device_id=(d, x_peer(k)), device_id_type=MESH)
    pl.semaphore_signal(barrier, inc=1, device_id=(d, sib), device_id_type=MESH)
    for c in fetch:
        c.wait()

    odd = core == 1

    @pl.when(f < 3)
    def _():
        at32 = act_t[...].astype(jnp.float32)
        gap = jnp.zeros((64, 128), jnp.float32)
        placed = jnp.where(odd, jnp.concatenate([gap, at32], 0), jnp.concatenate([at32, gap], 0))
        za[...] = placed.T.astype(jnp.bfloat16)

    pl.semaphore_wait(barrier, 22)

    h = lax.rem(xx, 2)

    def half_of(parity):
        return pl.ds(pl.multiple_of(64 * parity, 64), 64)

    def part(way):
        return pl.ds(pl.multiple_of(64 * h + 32 * way, 32), 32)

    def other_part(way):
        return pl.ds(pl.multiple_of(64 * (1 - h) + 32 * way, 32), 32)

    give_g = copy(gr, pan.at[1, d, :, pl.ds(0, 384)], s_p.at[0], r_p.at[2], (d, f + 1))
    give_z1 = copy(za, z1, s_p.at[0], r_p.at[0], (d, lax.rem(f + 31, 32)))
    give_t3 = copy(za.at[:, pl.ds(0, 128)], pan.at[0, d, :, pl.ds(384, 128)], s_p.at[0], r_p.at[1],
                   (d, lax.rem(f + 30, 32)))

    def own_x(k):
        rows = pl.ds(64 * (k % 2), 64)
        return copy(pan.at[core, d, rows], pan.at[core, d, rows], s_b.at[k], r_own, (d, x_peer(k)))

    def own_z(k):
        ref = pan.at[core, d, half_of(h)]
        return copy(ref, ref, s_c.at[k], r_own, (d, z_peer(k)))

    @pl.when(f == 0)
    def _():
        give_g.start()
        copy(za, z1, s_p.at[0], r_p.at[0], (d, f + 1)).wait_recv()
        pan[0, d, :, 0:128] = za[:, 0:128]
        pan[0, d, :, 128:256] = za[:, 128:256] + z1[:, 0:128]
        pan[0, d, :, 256:384] = z1[:, 128:256]
        copy(za.at[:, pl.ds(0, 128)], pan.at[0, d, :, pl.ds(384, 128)], s_p.at[0], r_p.at[1], (d, f + 1)).wait_recv()

    @pl.when(f == 1)
    def _():
        give_z1.start()
        pan[1, d, :, 384:512] = gr[:, 0:128]
        copy(gr, pan.at[1, d, :, pl.ds(0, 384)], s_p.at[0], r_p.at[2], (d, f + 1)).wait_recv()

    @pl.when(f == 2)
    def _():
        give_t3.start()

    @pl.when(f < 2)
    def _():
        for k in (1, 3, 2):
            own_x(k).start()

    @pl.when(jnp.logical_and(zh == 0, xx > 0))
    def _():
        own_z(1).wait_recv()

    @pl.when(zh == 0)
    def _():
        for k in (1, 3, 2):
            own_z(k).start()

    at32 = act_t[...].astype(jnp.float32)
    gt32 = gr[...].astype(jnp.float32).T
    for t in range(16):
        p, q = t // 8, t % 8
        low = at32[8 * q:8 * q + 8]
        mid = at32[64 + 8 * q:72 + 8 * q]
        top = at32[128 + 8 * q:136 + 8 * q]
        here = odd if p else jnp.logical_not(odd)
        fs[t, 0:16, :] = jnp.concatenate(
            [jnp.where(here, low, mid), jnp.where(here, top, mid)], 0).astype(jnp.bfloat16)
        gs = [gt32[128 * i + 8 * t:128 * i + 8 * t + 8] for i in range(3)]
        fs[t, 16:48, :] = jnp.concatenate(gs + [jnp.zeros_like(gs[0])], 0).astype(jnp.bfloat16)

    def features(k):
        to = lax.rem(d + k, 16)
        return copy(fs.at[to], feat.at[d], s_f.at[k], r_f.at[k], (to, f))

    for k in range(1, 16):
        features(k).start()
    feat[d] = fs[d]
    mat[...] = jnp.zeros_like(mat)
    invt[...] = jnp.zeros_like(invt)
    wmat[...] = jnp.zeros_like(wmat)
    raw[...] = jnp.zeros_like(raw)
    tables = owned_tables(own_ref, d, [f] + [z_peer(k) for k in range(1, 4)])

    @pl.when(zh > 0)
    def _():
        own_z(1).wait_recv()

    def at(dy, dz):
        return lax.rem(y + 4 - dy, 4) * 4 + lax.rem(zl + 4 - dz, 4)

    def y_dev(dy):
        return (lax.rem(y + dy, 4) * 4 + zl, f)

    def block(which, sem, to):
        ref = pan.at[core, which, half_of(h)]
        return copy(ref, ref, sem, r_blk.at[which], to)

    def z_copy(dz):
        return block(d, s_z.at[dz], (y * 4 + lax.rem(zl + dz, 4), f))

    def y_copy(dz, way):
        return block(at(0, dz), s_y.at[dz, way], y_dev((1, 3)[way]))

    def far_copy(dz, way):
        which = at((1, 3)[way], dz)
        ref = pan.at[core, which, part(way)]
        return copy(ref, ref, s_far.at[dz, way], r_far.at[way, which], y_dev((1, 3)[way]))

    def far_in(dz, way):
        which = at(2, dz)
        ref = pan.at[core, which, part(way)]
        return copy(ref, ref, s_far.at[dz, way], r_far.at[way, which], y_dev(1))

    def x_copy(dy, dz, way):
        which = at(dy, dz)
        ref = pan.at[core, which, part(way)]
        return copy(ref, ref, s_x.at[way, dy * 4 + dz], r_x.at[way, which], (d, x_peer((1, 3)[way])))

    def x_in(dy, dz, way):
        which = at(dy, dz)
        ref = pan.at[core, which, other_part(way)]
        return copy(ref, ref, s_x.at[way, 0], r_x.at[way, which], (d, x_peer(1)))

    holder = jnp.logical_and(zh == 0, xx == 0)

    def own_to_x(way, act):
        to_holder = jnp.logical_and(zh == 0, xx == (3, 1)[way])

        @pl.when(jnp.logical_not(to_holder))
        def _():
            act(x_copy(0, 0, way))

    def sibling(dy, dz):
        which = at(dy, dz)
        return copy(pan.at[core, which], pan.at[core, which], s_sib.at[dy * 4 + dz], r_sib.at[which], (d, sib))

    def whole(dy, dz):
        if dy or dz:
            for way in range(2):
                x_in(dy, dz, way).wait_recv()
        else:
            @pl.when(jnp.logical_not(holder))
            def _():
                for way in range(2):
                    x_in(dy, dz, way).wait_recv()
        sibling(dy, dz).start()

    def from_sibling(dy, dz):
        which = at(dy, dz)
        return copy(pan.at[1 - core, which], pan.at[1 - core, which], s_sib.at[1], r_sib.at[which], (d, sib))

    for dz in (1, 3, 2):
        z_copy(dz).start()
    for way in range(2):
        y_copy(0, way).start()
    for way in range(2):
        own_to_x(way, lambda c: c.start())
    for dz in (1, 3, 2):
        block(at(0, dz), s_z.at[dz], y_dev(1)).wait_recv()
        for way in range(2):
            y_copy(dz, way).start()
        for way in range(2):
            x_copy(0, dz, way).start()

    def line(dy):
        return pl.ds(pl.multiple_of(lax.rem(y + 4 - dy, 4) * 4, 4), 4)

    def ready(dy):
        for dz in range(4):
            from_sibling(dy, dz).wait_recv()

    def add_upper(n, cols, cols_t):
        mat[n, 0:256, 0:PANEL] = mat[n, 0:256, 0:PANEL] + dot16(cols_t[0:256], cols, ((1,), (0,)))
        mat[n, 256:PANEL, 256:PANEL] = mat[n, 256:PANEL, 256:PANEL] + dot16(
            cols_t[256:PANEL], cols[:, 256:PANEL], ((1,), (0,)))

    def sum_a(dy):
        pa = pan[0, line(dy)].reshape(512, PANEL)
        add_upper(0, pa, pa.T)

    def sum_g(dy):
        pg = pan[1, line(dy)].reshape(512, PANEL)
        add_upper(1, pg, pg.T)

    def sum_w(dy):
        pa = pan[0, line(dy)].reshape(512, PANEL)
        pg = pan[1, line(dy)].reshape(512, PANEL)
        wmat[...] = wmat[...] + dot16(pg.T, pa, ((1,), (0,)))

    def sum_rows(dy):
        ra = jnp.zeros((16, PANEL), jnp.float32)
        rg = jnp.zeros((32, PANEL), jnp.float32)
        for dz in range(4):
            which = at(dy, dz)
            ra = ra + dot16(feat[which, 0:16, :], pan[0, which], ((1,), (0,)))
            rg = rg + dot16(feat[which, 16:48, :], pan[1, which], ((1,), (0,)))
        raw[0:16, :] = raw[0:16, :] + ra
        raw[16:48, :] = raw[16:48, :] + rg

    def near(dz):
        for way in range(2):
            block(at((1, 3)[way], dz), s_z.at[1], y_dev(1)).wait_recv()
            far_copy(dz, way).start()
            for to in range(2):
                x_copy((1, 3)[way], dz, to).start()

    def far(dz):
        for way in range(2):
            far_in(dz, way).wait_recv()
            x_copy(2, dz, way).start()

    for dz in (0, 1, 3, 2):
        near(dz)
        whole(0, dz)
    far(0)
    ready(0)
    sum_a(0)
    far(1)
    for dz in (0, 1, 3, 2):
        whole(1, dz)
    sum_g(0)
    far(3)
    for dz in (0, 1, 3, 2):
        whole(3, dz)
    ready(1)
    sum_a(1)
    far(2)
    for k in range(1, 16):
        src = lax.rem(d + 16 - k, 16)
        copy(fs.at[d], feat.at[src], s_f.at[k], r_f.at[k], (lax.rem(d + 1, 16), f)).wait_recv()
    sum_rows(0)
    sum_g(1)
    for dz in (0, 1, 3, 2):
        whole(2, dz)
    sum_rows(1)
    ready(3)
    sum_a(3)
    sum_rows(3)
    ready(2)
    sum_rows(2)

    for s in range(GROUPS):
        loc[role, s] = raw[8 * s:8 * s + 8, :] * scale

    def l_x(k):
        return copy(loc.at[role], loc.at[role], s_lx.at[k], r_l.at[role], (d, x_peer(k)))

    def l_role(k):
        return 2 * lax.rem(xx + k, 4) + core

    def l_sib(k):
        r = l_role(k)
        return copy(loc.at[r], loc.at[r], s_ls.at[k], r_l.at[r], (d, sib))

    def l_in(r):
        return copy(loc.at[r], loc.at[r], s_ls.at[0], r_l.at[r], (d, sib))

    def slots(k):
        return copy(pack.at[k], got.at[zh], s_g.at[k], r_g.at[zh], (d, z_peer(k)))

    for k in (1, 3, 2):
        l_x(k).start()
    l_sib(0).start()

    sum_g(3)
    for k in (1, 3, 2):
        l_in(l_role(k)).wait_recv()
        l_sib(k).start()
    sum_a(2)
    sum_g(2)
    for k in range(4):
        l_in(l_role(k) + 1 - 2 * core).wait_recv()
    for k in (1, 3, 2):
        for s in range(CAP):
            place = tables[k][s]
            pack[k, s] = loc[lax.rem(place[0], 8), place[1]]
        slots(k).start()
    for s in range(CAP):
        place = tables[0][s]
        got[zh, s] = loc[lax.rem(place[0], 8), place[1]]

    eye = jnp.where(lax.broadcasted_iota(jnp.int32, (BLK, BLK), 0) == lax.broadcasted_iota(jnp.int32, (BLK, BLK), 1),
                    jnp.float32(damping), jnp.float32(0.0))

    def block_at(n, i, j, width=BLK):
        b = mat[n, i * BLK:(i + 1) * BLK, j * BLK:j * BLK + width] * scale
        if i == j:
            diag = b[:, 0:BLK] + eye
            b = diag if width == BLK else jnp.concatenate([diag, b[:, BLK:]], 1)
        return b

    for n in range(2):
        for i in range(4):
            mat[n, i * BLK:(i + 1) * BLK, i * BLK:PANEL] = block_at(n, i, i, PANEL - i * BLK)

    x = mat[:, 0:BLK, 0:BLK]
    for kk in range(4):
        lo, hi = kk * BLK, (kk + 1) * BLK
        factor_blocks(x, inv0.at[kk])
        sum_w(kk)
        li = [inv0[kk, n] for n in range(2)]
        if kk < 3:
            first = [dot32(li[n], mat[n, lo:hi, hi:hi + BLK], ((1,), (0,))) for n in range(2)]
            first_t = [v.T for v in first]
            x = jnp.stack([
                mat[n, hi:hi + BLK, hi:hi + BLK] - dot32(first_t[n], first[n], ((1,), (0,))) for n in range(2)])
        for n in range(2):
            mat[n, lo:hi, PANEL + lo:PANEL + hi] = li[n]
            if kk < 3:
                rest = PANEL + lo - hi - BLK
                if rest:
                    mat[n, lo:hi, hi + BLK:PANEL + lo] = dot32(li[n], mat[n, lo:hi, hi + BLK:PANEL + lo], ((1,), (0,)))
                row = mat[n, lo:hi, hi + BLK:PANEL + hi]
                mat[n, hi:hi + BLK, hi + BLK:PANEL + hi] = mat[n, hi:hi + BLK, hi + BLK:PANEL + hi] - dot32(
                    first_t[n], row, ((1,), (0,)))
                for i in range(kk + 2, 4):
                    ut = mat[n, lo:hi, i * BLK:(i + 1) * BLK].T
                    mat[n, i * BLK:(i + 1) * BLK, i * BLK:PANEL + hi] = mat[
                        n, i * BLK:(i + 1) * BLK, i * BLK:PANEL + hi] - dot32(
                        ut, mat[n, lo:hi, i * BLK:PANEL + hi], ((1,), (0,)))
            elif kk == 3:
                mat[n, lo:hi, PANEL:PANEL + lo] = dot32(li[n], mat[n, lo:hi, PANEL:PANEL + lo], ((1,), (0,)))
            invt[n, 0:hi, lo:hi] = mat[n, lo:hi, PANEL:PANEL + hi].T

    mine = pl.multiple_of(f * 16, 16)
    picked[8 * CAP:, :] = dot32(mat[1, pl.ds(mine, 16), PANEL:] * scale, wmat[...], ((1,), (0,)))
    for k in range(1, 4):
        src = lax.rem(zh + k, 4)
        copy(pack.at[k], got.at[src], s_g.at[k], r_g.at[src], (d, z_peer(k))).wait_recv()
    table = tables[0]
    for s in range(CAP):
        picked[8 * s:8 * s + 8, :] = got[lax.div(table[s][0], 8), s]
    def times_inverse(n, rows):
        left = dot32(rows[:, 0:256], invt[n, 0:256, 0:256], ((1,), (0,)))
        return jnp.concatenate([left, dot32(rows, invt[n, :, 256:PANEL], ((1,), (0,)))], 1)

    ra = times_inverse(0, picked[...])
    rg = times_inverse(1, picked[0:8 * CAP, :])
    pre_out[...] = ra[8 * CAP:, :]
    for s in range(CAP):
        lo, hi = 8 * s, 8 * s + 8
        out = jnp.where(jnp.full((8, PANEL), table[s][2]) == 1, ra[lo:hi, :], rg[lo:hi, :])
        rows_out[s] = jnp.where(jnp.full((8, PANEL), table[s][3]) == 1, out, 0.0)

    @pl.when(f == 0)
    def _():
        give_g.wait_send()

    @pl.when(f == 1)
    def _():
        give_z1.wait_send()

    @pl.when(f == 2)
    def _():
        give_t3.wait_send()

    @pl.when(f < 2)
    def _():
        for k in (1, 2, 3):
            own_x(k).wait_send()

    @pl.when(zh == 0)
    def _():
        for k in (1, 2, 3):
            own_z(k).wait_send()

    for way in range(2):
        own_to_x(way, lambda c: c.wait_send())
    for k in range(1, 16):
        features(k).wait_send()
        for way in range(2):
            x_copy(k // 4, k % 4, way).wait_send()
    for k in range(16):
        sibling(k // 4, k % 4).wait_send()
    for k in (1, 2, 3):
        z_copy(k).wait_send()
        l_x(k).wait_send()
        slots(k).wait_send()
    for dz in range(4):
        for way in range(2):
            y_copy(dz, way).wait_send()
            far_copy(dz, way).wait_send()
        l_sib(dz).wait_send()


def window(owners, acts_t, grads_out):
    vmem = pl.BlockSpec(memory_space=pltpu.VMEM)
    dma = pltpu.SemaphoreType.DMA
    f32, bf16 = jnp.float32, jnp.bfloat16
    return pl.pallas_call(
        kernel,
        out_shape=(
            jax.ShapeDtypeStruct((CAP, 8, PANEL), f32),
            jax.ShapeDtypeStruct((16, PANEL), f32),
        ),
        in_specs=[pl.BlockSpec(memory_space=pltpu.HBM)] * 3,
        out_specs=(vmem, vmem),
        scratch_shapes=[
            pltpu.SMEM((NT,), jnp.int32),
            pltpu.VMEM((192, 128), bf16),
            pltpu.VMEM((128, 384), bf16),
            pltpu.VMEM((16, FROWS, 128), bf16),
            pltpu.VMEM((128, 256), bf16),
            pltpu.VMEM((2, 16, 128, PANEL), bf16),
            pltpu.VMEM((16, FROWS, 128), bf16),
            pltpu.VMEM((128, 256), bf16),
            pltpu.VMEM((2, PANEL, 2 * PANEL), f32),
            pltpu.VMEM((4, 2, BLK, BLK), f32),
            pltpu.VMEM((2, PANEL, PANEL), f32),
            pltpu.VMEM((PANEL, PANEL), f32),
            pltpu.VMEM((FROWS, PANEL), f32),
            pltpu.VMEM((8, GROUPS, 8, PANEL), f32),
            pltpu.VMEM((4, CAP, 8, PANEL), f32),
            pltpu.VMEM((4, CAP, 8, PANEL), f32),
            pltpu.VMEM((8 * CAP + 16, PANEL), f32),
            dma((3,)),
            dma((1,)), dma((3,)), dma((4,)), dma((4,)), dma,
            dma((4,)), dma((16,)), dma((4, 2)),
            dma((4, 2)), dma((2, 16)),
            dma((2, 16)), dma((2, 16)),
            dma((16,)), dma((16,)),
            dma((16,)), dma((16,)),
            dma((4,)), dma((4,)), dma((8,)),
            dma((4,)), dma((4,)),
        ],
        compiler_params=pltpu.CompilerParams(
            collective_id=0, has_side_effects=True, vmem_limit_bytes=60 * 2**20),
        name="window",
    )(owners, acts_t, grads_out)


def on_device(acts, grads_out, owners):
    rows, pre = window(owners, acts.T, grads_out)
    return rows[None], pre


def solution(mesh):
    return jax.shard_map(
        on_device,
        mesh=mesh,
        in_specs=(P("dp", "factor"), P("dp", "factor"), P()),
        out_specs=(P("factor", None, "dp", None), P("factor", None)),
        check_vma=False,
    )
```

profile of v0, /device:TPU:1, one launch (start us, length us, event | category | flops | bytes accessed | tf_op | source)
XLA Modules:
  0.0 94.1 jit_solution(9081908364373502008)
XLA Ops:
  0.6 91.2 %window.1 = (f32[6,8,512]{2,1,0:T(8,128)}, f32[16,512]{1,0:T(8,128)}) custom-call(s32[136]{0:T(256)} %own_in.1, bf16[192,128]{1,0:T(8,128)(2,1)} %bitcast.3, bf16[128,384]{1,0:T(8,128)(2,1)} %gr_in.1), custom_call_target="tpu_custom_call" | custom-call | tf_op jit(solution)/shard_map/window/pallas_call | solution.py:605
  91.9 0.0 copy-start
  91.9 1.5 %copy.7 = f32[1,6,8,512]{3,2,1,0:T(8,128)} copy(f32[1,6,8,512]{3,2,1,0:T(8,128)} %bitcast.2) | data formatting | bytes 196608
  93.4 0.0 copy-done
  93.4 0.6 copy.8
Async XLA Ops:
  91.9 1.6 %copy-start = (f32[16,512]{1,0:T(8,128)S(1)}, f32[16,512]{1,0:T(8,128)}, u32[]{:S(2)}) copy-start(f32[16,512]{1,0:T(8,128)} %get-tuple-element.9) | copy-start | bytes 98308
where the time goes:
time: 94.2 us; the launch traced here: 94.1 us
  Pallas kernels  91.2 us (97%)
  local copies, waits for them, and re-layouts  2.16 us (2%)
    pallas_call x1, Pallas kernels, window(): pl.pallas_call(kernel, out_shape=(jax.ShapeDtypeStruct((CAP, 8, PANEL), f...  91.2 us
    unnamed x4, local copies, waits for them, and re-layouts  2.16 us

commit v1 on v0

--- a/solution.py
+++ b/solution.py
@@ -42,7 +42,7 @@
 
 
 def strip16(x0, x1, w0, w1, c0, sub):
-    b0 = [lanes(x0, c0 + j) for j in range(16)]
+    b0 = [lanes(x0, c0 + j) for j in range(8)]
     b1 = [lanes(x1, c0 + j) for j in range(16)]
     d0 = jnp.ones(x0.shape, jnp.float32)
     d1 = d0
@@ -55,10 +55,14 @@
         m0b = jnp.where(sub > j + 1, bb * p00 - ba * p01, 0.0) * rd
         m1a = b1[j] * r0
         m1b = (b1[j + 1] * p00 - b1[j] * p01) * rd
-        for k in range(j + 2, 16):
+        for k in range(j + 2, 8):
             ra = rows8(b0[k], j)
             rb = rows8(b0[k], j + 1) - q * ra
             b0[k] = b0[k] - m0a * ra - m0b * rb
+            b1[k] = b1[k] - m1a * ra - m1b * rb
+        for k in range(8, 16):
+            ra = rows8(b1[j], k - 8)
+            rb = rows8(b1[j + 1], k - 8) - q * ra
             b1[k] = b1[k] - m1a * ra - m1b * rb
         ra = rows8(x0, j)
         rb = rows8(x0, j + 1) - q * ra
@@ -391,16 +395,13 @@
 
     def sum_a(dy):
         pa = pan[0, line(dy)].reshape(512, PANEL)
-        add_upper(0, pa, pa.T)
+        pat = pa.T
+        add_upper(0, pa, pat)
+        wmat[...] = wmat[...] + dot16(pat, pan[1, line(dy)].reshape(512, PANEL), ((1,), (0,)))
 
     def sum_g(dy):
         pg = pan[1, line(dy)].reshape(512, PANEL)
         add_upper(1, pg, pg.T)
-
-    def sum_w(dy):
-        pa = pan[0, line(dy)].reshape(512, PANEL)
-        pg = pan[1, line(dy)].reshape(512, PANEL)
-        wmat[...] = wmat[...] + dot16(pg.T, pa, ((1,), (0,)))
 
     def sum_rows(dy):
         ra = jnp.zeros((16, PANEL), jnp.float32)
@@ -512,7 +513,6 @@
     for kk in range(4):
         lo, hi = kk * BLK, (kk + 1) * BLK
         factor_blocks(x, inv0.at[kk])
-        sum_w(kk)
         li = [inv0[kk, n] for n in range(2)]
         if kk < 3:
             first = [dot32(li[n], mat[n, lo:hi, hi:hi + BLK], ((1,), (0,))) for n in range(2)]
@@ -538,7 +538,8 @@
             invt[n, 0:hi, lo:hi] = mat[n, lo:hi, PANEL:PANEL + hi].T
 
     mine = pl.multiple_of(f * 16, 16)
-    picked[8 * CAP:, :] = dot32(mat[1, pl.ds(mine, 16), PANEL:] * scale, wmat[...], ((1,), (0,)))
+    mine_t = (mat[1, pl.ds(mine, 16), PANEL:] * scale).T
+    picked[8 * CAP:, :] = dot32(wmat[...], mine_t, ((1,), (0,))).T
     for k in range(1, 4):
         src = lax.rem(zh + k, 4)
         copy(pack.at[k], got.at[src], s_g.at[k], r_g.at[src], (d, z_peer(k))).wait_recv()

time: 94.2 us -> 92.8 us (0.985)
  Pallas kernels: 91.2 us -> 89.8 us
    pallas_call x1, Pallas kernels: 91.2 us -> 89.8 us  [window(): pl.pallas_call(kernel, out_shape=(jax.ShapeDtypeStruct((CAP, 8, PANEL), f...]
where the time goes in v1:
time: 92.8 us; the launch traced here: 92.6 us
  Pallas kernels  89.8 us (97%)
  local copies, waits for them, and re-layouts  2.16 us (2%)
    pallas_call x1, Pallas kernels, window(): pl.pallas_call(kernel, out_shape=(jax.ShapeDtypeStruct((CAP, 8, PANEL), f...  89.8 us
    unnamed x4, local copies, waits for them, and re-layouts  2.16 us

profile of v1, /device:TPU:1, one launch (start us, length us, event | category | flops | bytes accessed | tf_op | source)
XLA Modules:
  0.0 92.6 jit_solution(6946722643315159519)
XLA Ops:
  0.6 89.8 %window.1 = (f32[6,8,512]{2,1,0:T(8,128)}, f32[16,512]{1,0:T(8,128)}) custom-call(s32[136]{0:T(256)} %own_in.1, bf16[192,128]{1,0:T(8,128)(2,1)} %bitcast.3, bf16[128,384]{1,0:T(8,128)(2,1)} %gr_in.1), custom_call_target="tpu_custom_call" | custom-call | tf_op jit(solution)/shard_map/window/pallas_call | solution.py:606
  90.4 0.0 copy-start
  90.4 1.5 %copy.7 = f32[1,6,8,512]{3,2,1,0:T(8,128)} copy(f32[1,6,8,512]{3,2,1,0:T(8,128)} %bitcast.2) | data formatting | bytes 196608
  92.0 0.0 copy-done
  92.0 0.6 copy.8
Async XLA Ops:
  90.4 1.6 %copy-start = (f32[16,512]{1,0:T(8,128)S(1)}, f32[16,512]{1,0:T(8,128)}, u32[]{:S(2)}) copy-start(f32[16,512]{1,0:T(8,128)} %get-tuple-element.9) | copy-start | bytes 98308
